TPU v7x, 32 devices: a whole 2x2x4 slice. The times are simulated.
32 devices in a mesh: gx: 4 (over z), gy: 4 (over y, x), gz: 2 (over core).
Axes of the slice: x: 2, y: 2, z: 4, core: 2. Of those that a mesh axis runs over, the one named last changes fastest.
Arguments:
- points: float32 [1024, 3, 128], P(('gx', 'gy', 'gz')), may hold values from -6 to 6
- source: float32 [1024, 128], P(('gx', 'gy', 'gz')), may hold values from -6 to 6
- density: float32 [1024, 128], P(('gx', 'gy', 'gz')), may hold values from -3 to 3
- anterp: bfloat16 [1024, 216, 128], P(('gx', 'gy', 'gz')), may hold values from -0.5 to 0.5
- child_slot: int32 [1024], P(('gx', 'gy', 'gz')), may hold values from 0 to 7, as said below
- child_ops: bfloat16 [8, 216, 216], replicated, may hold values from -0.4375 to 0.4375
- parent: int32 [1024], P(('gx', 'gy', 'gz')), may hold values from 0 to 127, as said below
- near_list: int32 [1024, 27], P(('gx', 'gy', 'gz')), may hold values from -1 to 1023, as said below
- far_list: int32 [128, 189], P(('gx', 'gy', 'gz')), may hold values from 0 to 127
- far_op: int32 [128, 189], P(('gx', 'gy', 'gz')), may hold values from 0 to 15
- translations: bfloat16 [16, 216, 216], replicated, may hold values from -0.03125 to 0.03125
Outputs:
- density_out: float32 [1024, 128], P(('gx', 'gy', 'gz'))
- potential: float32 [1024, 128], P(('gx', 'gy', 'gz'))
Inputs may be any that keep to these rules, and one draw needn't show every extreme that they name: Every octant has exactly 8 child leaves. Leaf l of device d = l // 32 has a parent octant owned by d or by a device next to d along gz with the same gx and gy index: parent // 4 is d - 1, d or d + 1, never past the ends of gz. `child_slot`: the 8 children of one octant have 8 different positions. `near_list`: row l lists distinct leaves: entry 0 is l itself, then other leaves b with |b - l| <= 13 on devices with the same gx and gy index as l's, then -1 in the remaining slots; at least 9 entries are listed.
All inputs are finite; a program needn't handle non-finite values.
Results may differ from a plain program's by a relative error of at most 0.008.
Values may be sent and summed in bfloat16 or wider, within the bound.
No kernel may reach another device: no remote copies, remote signals or barrier semaphores. Data moves between devices by JAX's collectives and lax.ppermute only.
A program may use at most 64 MiB of HBM per device.

v0:
```python
import functools

import jax
import jax.numpy as jnp
from jax import lax
from jax.experimental import pallas as pl
from jax.experimental.pallas import tpu as pltpu
from jax.sharding import PartitionSpec as P

AXES = ("gx", "gy", "gz")
GHOST = 13
ITERS = 2
CHILDREN = 8

SOFTEN = 0.01
DAMPING = 0.5
FAR_WEIGHT = 0.3
NEAR_WEIGHT = 0.03

BF16 = jnp.bfloat16
F32 = jnp.float32
UNROLL = 8
M2L_LOOP = 2
L2L_LOOP = 2
CHUNKS = 2
LATER_MIB = 6
NT = (((1,), (1,)), ((), ()))
VMEM = pl.BlockSpec(memory_space=pltpu.VMEM)
SMEM = pl.BlockSpec(memory_space=pltpu.SMEM)
HBM = pl.BlockSpec(memory_space=pltpu.HBM)


def in_hbm(array):
    return pltpu.with_memory_space_constraint(array, pltpu.HBM)


def dot(a, b):
    return jnp.dot(a, b, preferred_element_type=F32)


def dot_nt(a, b):
    return lax.dot_general(a, b, NT, preferred_element_type=F32)


def three_parts(x):
    high = x.astype(BF16).astype(F32)
    rest = x - high
    middle = rest.astype(BF16).astype(F32)
    return high, middle, rest - middle


def features(x):
    row = lax.broadcasted_iota(jnp.int32, x.shape, 0)
    high, middle, low = three_parts(x)
    norm = jnp.broadcast_to(jnp.sum(x * x, axis=0, keepdims=True), x.shape)
    nh, nm, nl = three_parts(norm)
    eh, em, el = three_parts(norm + SOFTEN)
    zero = jnp.zeros_like(x)
    last = jnp.where(row < 6, 1.0, 0.0)
    source_norm = jnp.where(row == 0, nh, jnp.where(row == 1, nm, jnp.where(row == 2, nl, last)))
    first = jnp.where(row < 3, 1.0, 0.0)
    target_norm = jnp.where(row == 3, eh, jnp.where(row == 4, em, jnp.where(row == 5, el, first)))
    source = [high, high, middle, middle, high, low, source_norm, zero]
    target = [-2 * high, -2 * middle, -2 * high, -2 * middle, -2 * low, -2 * high, target_norm, zero]
    return jnp.concatenate(source, 0), jnp.concatenate(target, 0)


def coordinates(points_ref, leaf):
    x, y, z = [points_ref[c, pl.ds(leaf, 1), :] for c in range(3)]
    row = lax.broadcasted_iota(jnp.int32, (8, x.shape[1]), 0)
    return jnp.where(row == 0, x, jnp.where(row == 1, y, jnp.where(row == 2, z, 0.0)))


def other_row(pair, low, leaf, leaves):
    return jnp.where(low, leaf, leaves - 1 - leaf) if pair else leaf


def near_part(
    pair, first, count, listed_ref, points_ref, points_other_ref, q_ref, q_other_ref, out_ref,
    source_s, target_s, q_s, ahead_s, back_s,
):
    leaves, width = out_ref.shape
    reach = GHOST + 1
    stop = first + count
    end = stop + GHOST
    low = lax.axis_index("gz") == 0 if pair else True

    def place(i):
        return jnp.where(low, i, leaves - 1 - i) if pair else i

    def own(i, carry):
        leaf = place(i)
        source, target = features(coordinates(points_ref, leaf))
        source_s[i] = source.astype(BF16)
        target_s[i] = target.T.astype(BF16)
        q_s[pl.ds(i, 1), :] = q_ref[pl.ds(leaf, 1), :]
        return carry

    def own_source(i, carry):
        leaf = place(i)
        source_s[i] = features(coordinates(points_ref, leaf))[0].astype(BF16)
        q_s[pl.ds(i, 1), :] = q_ref[pl.ds(leaf, 1), :]
        return carry

    def other(i, carry):
        leaf = other_row(pair, low, i, leaves)
        source_s[leaves + i] = features(coordinates(points_other_ref, leaf))[0].astype(BF16)
        q_s[pl.ds(leaves + i, 1), :] = q_other_ref[pl.ds(leaf, 1), :]
        return carry

    lax.fori_loop(first, stop, own, 0, unroll=4)
    lax.fori_loop(stop, min(end, leaves), own_source, 0, unroll=4)
    lax.fori_loop(0, max(end - leaves, 0), other, 0, unroll=4)

    def target(i, carry):
        rows = target_s[i]
        mine = jnp.broadcast_to(q_s[pl.ds(i, 1), :], (width, width)).T
        acc = jnp.zeros((width, width), F32)
        for d in range(0, reach, 2):
            sources = [source_s[i + d], source_s[i + d + 1]]
            tiles = lax.rsqrt(dot(rows, jnp.concatenate(sources, 1)))
            for part in (0, 1):
                shift = d + part
                tile = tiles[:, part * width : (part + 1) * width]
                acc = acc + tile * (q_s[pl.ds(i + shift, 1), :] * listed_ref[place(i), i + shift])
                if shift:
                    inside = i + shift < leaves
                    weight = listed_ref[place(jnp.minimum(i + shift, leaves - 1)), i]
                    weight = jnp.where(inside, weight, 0.0)
                    back = jnp.sum((tile * mine).reshape(width // 8, 8, width), axis=0)
                    back_s[i + shift, shift - 1] = back * weight
        ahead_s[i] = jnp.sum(acc.T.reshape(width // 8, 8, width), axis=0)
        return carry

    lax.fori_loop(first, stop, target, 0, unroll=min(count, UNROLL))

    if not pair and first == 0:
        halo = q_other_ref.shape[0] // 2
        lax.fori_loop(halo, 2 * halo, other, 0)

        def behind(i, carry):
            acc = jnp.zeros((width, width), F32)
            for j in range(leaves + halo, leaves + 2 * halo):
                tile = lax.rsqrt(dot(target_s[i], source_s[j]))
                acc = acc + tile * (q_s[j : j + 1] * listed_ref[i, j])
            ahead_s[i] = ahead_s[i] + jnp.sum(acc.T.reshape(width // 8, 8, width), axis=0)
            return carry

        lax.fori_loop(0, GHOST, behind, 0)

    for i in range(first, min(end, leaves)):
        terms = [ahead_s[i]] if i < stop else []
        terms += [back_s[i, d - 1] for d in range(1, reach) if first <= i - d < stop]
        total = functools.reduce(jnp.add, terms)
        row = pl.ds(place(i), 1)
        out_ref[row, :] = out_ref[row, :] + jnp.sum(total, axis=0, keepdims=True)


def near_scratch(leaves, rows, width):
    return [
        pltpu.VMEM((rows, 64, width), BF16),
        pltpu.VMEM((leaves, width, 64), BF16),
        pltpu.VMEM((rows, width), F32),
        pltpu.VMEM((leaves, 8, width), F32),
        pltpu.VMEM((leaves + GHOST, GHOST, 8, width), F32),
    ]


def near_kernel(
    pair, count, listed_ref, points_ref, points_other_ref, q_ref, q_other_ref, out_ref,
    source_s, target_s, q_s, ahead_s, back_s,
):
    out_ref[...] = jnp.zeros_like(out_ref)
    near_part(
        pair, 0, count, listed_ref, points_ref, points_other_ref, q_ref, q_other_ref, out_ref,
        source_s, target_s, q_s, ahead_s, back_s,
    )


def near_start(pair, count, listed, points, points_other, q, q_other):
    leaves, width = q.shape
    pairs = count * (GHOST + 1) * width * width
    return pl.pallas_call(
        functools.partial(near_kernel, pair, count),
        out_shape=jax.ShapeDtypeStruct((leaves, width), F32),
        in_specs=[SMEM, VMEM, VMEM, VMEM, VMEM],
        out_specs=VMEM,
        scratch_shapes=near_scratch(leaves, listed.shape[1], width),
        compiler_params=params(6),
        cost_estimate=pl.CostEstimate(flops=pairs * 8192, bytes_accessed=1 << 20, transcendentals=pairs),
        name="near_start",
    )(listed, points, points_other, q, q_other)


def leaf_codes(pair, octs, slots, child_slot_ref, parent_ref):
    device = lax.axis_index(AXES)
    first = (device // 2 * 2 if pair else device - 1) * octs
    return child_slot_ref[...] * slots + (parent_ref[...] - first)


def child_rows(code, rows):
    index = lax.broadcasted_iota(jnp.int32, (rows, code.shape[1]), 0)
    return jnp.where(index == code, 1.0, 0.0).astype(BF16)


def leaf_multipoles(by_point, anterp_ref, first, count):
    lane = lax.broadcasted_iota(jnp.int32, by_point.shape, 1)
    mult = jnp.zeros((anterp_ref.shape[1], by_point.shape[1]), F32)
    for leaf in range(0, count, 2):
        maps = jnp.concatenate([anterp_ref[first + leaf], anterp_ref[first + leaf + 1]], 1)
        values = [jnp.where(lane == first + leaf + i, by_point, 0.0) for i in (0, 1)]
        mult = mult + dot(maps, jnp.concatenate(values, 0))
    return mult


def octant_parts(mult, code, child_ref, table_ref):
    devices, slots, nodes = table_ref.shape
    columns = CHILDREN * slots
    by_child = dot_nt(mult.astype(BF16), child_rows(code, columns)).astype(BF16)
    position = lax.broadcasted_iota(jnp.int32, by_child.shape, 1) // slots
    part = jnp.zeros((nodes, columns), F32)
    for child in range(CHILDREN):
        part = part + dot(child_ref[child], jnp.where(position == child, by_child, 0.0))
    part = jnp.sum(part.T.reshape(CHILDREN, slots, nodes), axis=0).astype(BF16)
    for device in range(devices):
        table_ref[device] = part


def downward(tables_ref, counts_ref, trans_ref, code, anterp_ref, child_ref, grouped_s, back_s, maps_ready):
    devices, slots, nodes = tables_ref.shape
    leaves = anterp_ref.shape[0]
    ops = trans_ref.shape[0]
    tables = tables_ref[...].reshape(devices * slots, nodes)
    grouped_s[...] = dot(counts_ref[...], tables).reshape(ops, slots, nodes)

    def translate(i, local):
        for j in range(ops // M2L_LOOP):
            op = i * (ops // M2L_LOOP) + j
            local = local + dot_nt(grouped_s[op].astype(BF16), trans_ref[op])
        return local

    local = lax.fori_loop(0, M2L_LOOP, translate, jnp.zeros((slots, nodes), F32)).astype(BF16)

    def to_children(i, carry):
        for j in range(CHILDREN // L2L_LOOP):
            child = i * (CHILDREN // L2L_LOOP) + j
            back_s[child] = dot(local, child_ref[child])
        return carry

    lax.fori_loop(0, L2L_LOOP, to_children, 0)
    back = back_s[...].reshape(CHILDREN * slots, nodes).astype(BF16)
    pick = child_rows(code, CHILDREN * slots)
    leaf_local = lax.dot_general(pick, back, (((0,), (0,)), ((), ())), preferred_element_type=F32)
    leaf_local = leaf_local.astype(BF16)
    maps_ready()
    far = [dot(leaf_local[leaf : leaf + 1], anterp_ref[leaf]) for leaf in range(leaves)]
    return jnp.concatenate(far, 0)


def update(density, source, far, near):
    potential = FAR_WEIGHT * far + NEAR_WEIGHT * near
    return density + DAMPING * (jnp.tanh(source - potential) - density), potential


def fetch(hbm, vmem, sem):
    copy = pltpu.make_async_copy(hbm, vmem, sem)
    copy.start()
    return copy


def first_kernel(
    pair, octs, q_hbm, child_slot_hbm, parent_hbm, anterp_hbm, child_hbm, table_ref,
    q_s, child_slot_s, parent_s, anterp_s, child_s, sems,
):
    small = [
        fetch(q_hbm, q_s, sems.at[0]),
        fetch(child_slot_hbm, child_slot_s, sems.at[1]),
        fetch(parent_hbm, parent_s, sems.at[2]),
    ]
    chunk = anterp_s.shape[0] // CHUNKS

    def maps(i):
        part = pl.ds(i * chunk, chunk)
        return pltpu.make_async_copy(anterp_hbm.at[part], anterp_s.at[part], sems.at[4 + i])

    for i in range(CHUNKS):
        maps(i).start()
    child = fetch(child_hbm, child_s, sems.at[3])
    for copy in small:
        copy.wait()
    code = leaf_codes(pair, octs, table_ref.shape[1], child_slot_s, parent_s)
    by_point = q_s[...].T.astype(BF16)

    def take(i, mult):
        maps(i).wait()
        return mult + leaf_multipoles(by_point, anterp_s, i * chunk, chunk)

    mult = lax.fori_loop(0, CHUNKS, take, jnp.zeros((anterp_s.shape[1], anterp_s.shape[0]), F32))
    child.wait()
    octant_parts(mult, code, child_s, table_ref)


def later_kernel(
    pair, octs, last, near_ref, tables_ref, counts_ref, source_ref, q_ref, child_slot_ref, parent_ref, trans_ref,
    child_ref, anterp_hbm, new_q_ref, other_out_ref, anterp_s, grouped_s, back_s, sem,
):
    maps = fetch(anterp_hbm, anterp_s, sem)
    code = leaf_codes(pair, octs, tables_ref.shape[1], child_slot_ref, parent_ref)
    far = downward(tables_ref, counts_ref, trans_ref, code, anterp_s, child_ref, grouped_s, back_s, maps.wait)
    new_q, potential = update(q_ref[...], source_ref[...], far, near_ref[...])
    new_q_ref[...] = new_q
    if last:
        other_out_ref[...] = potential
    else:
        mult = leaf_multipoles(new_q.T.astype(BF16), anterp_s, 0, anterp_s.shape[0])
        octant_parts(mult, code, child_ref, other_out_ref)


def counts_kernel(pair, octs, far_list_ref, far_op_ref, counts_ref, rows_s):
    slots, inter = far_list_ref.shape
    rows, columns = counts_ref.shape
    ops = rows // slots
    column = lax.broadcasted_iota(jnp.int32, (columns, inter), 0)
    device, slot = column // slots, column % slots
    octant = (device // 2 * 2 if pair else device - 1) * octs + slot
    op = lax.broadcasted_iota(jnp.int32, (ops, inter), 0)
    for g in range(slots):
        source = jnp.where(octant == far_list_ref[g : g + 1], 1.0, 0.0).astype(BF16)
        chosen = jnp.where(op == far_op_ref[g : g + 1], 1.0, 0.0).astype(BF16)
        rows_s[:, g, :] = dot_nt(chosen, source)
    counts_ref[...] = rows_s[...].reshape(rows, columns).astype(BF16)


def params(mib=4):
    return pltpu.CompilerParams(vmem_limit_bytes=mib << 20)


def swap(array):
    return lax.ppermute(array, "gz", [(0, 1), (1, 0)])


def beside(array, axis, width):
    count = lax.axis_size("gz")
    if count == 2:
        return swap(array)
    length = array.shape[axis]
    up = [(i, i + 1) for i in range(count - 1)]
    down = [(i + 1, i) for i in range(count - 1)]
    after = lax.ppermute(lax.slice_in_dim(array, 0, width, axis=axis), "gz", down)
    before = lax.ppermute(lax.slice_in_dim(array, length - width, length, axis=axis), "gz", up)
    return jnp.concatenate([after, before], axis)


def listed_pairs(near_list, device, pair, rows, halo):
    leaves = near_list.shape[0]
    row = jnp.arange(rows, dtype=jnp.int32)
    if pair:
        leaf = jnp.where(lax.axis_index("gz") == 0, row, leaves - 1 - row)
    else:
        leaf = jnp.where(row < leaves + halo, row, row - rows)
    leaf = leaf + device * leaves
    return jnp.any(near_list[:, :, None] == leaf[None, None, :], axis=1).astype(F32)


def octant_window(array):
    count = lax.axis_size("gz")
    if count == 2:
        other = swap(array)
        low = lax.axis_index("gz") == 0
        return jnp.where(low, jnp.concatenate([array, other], 0), jnp.concatenate([other, array], 0))
    up = [(i, i + 1) for i in range(count - 1)]
    down = [(i + 1, i) for i in range(count - 1)]
    rows = [lax.ppermute(array, "gz", up), array, lax.ppermute(array, "gz", down)]
    rows = jnp.concatenate(rows, 0)
    return jnp.pad(rows, ((0, -rows.shape[0] % 8), (0, 0)))


def shards(
    points, source, density, anterp, child_slot, child_ops, parent, near_list, far_list, far_op, translations
):
    leaves, _, width = points.shape
    octs, inter = far_list.shape
    ops, nodes, _ = translations.shape
    devices = lax.axis_size(AXES)
    pair = lax.axis_size("gz") == 2
    device = lax.axis_index(AXES)
    halo = -(-GHOST // 8) * 8

    child_row, parent_row = child_slot[None, :], parent[None, :]
    slots = -(-(2 if pair else 3) * octs // 8) * 8
    table_shape = jax.ShapeDtypeStruct((devices, slots, nodes), BF16)
    field_shape = jax.ShapeDtypeStruct((leaves, width), F32)
    table = pl.pallas_call(
        functools.partial(first_kernel, pair, octs),
        out_shape=table_shape,
        in_specs=[HBM] * 5,
        out_specs=VMEM,
        scratch_shapes=[
            pltpu.VMEM(density.shape, F32),
            pltpu.VMEM(child_row.shape, jnp.int32),
            pltpu.VMEM(parent_row.shape, jnp.int32),
            pltpu.VMEM(anterp.shape, BF16),
            pltpu.VMEM(child_ops.shape, BF16),
            pltpu.SemaphoreType.DMA((8,)),
        ],
        compiler_params=params(8),
        name="upward_pass",
    )(*map(in_hbm, (density, child_row, parent_row, anterp, child_ops)))

    points, far_list, far_op, near_list, table = lax.optimization_barrier(
        (points, far_list, far_op, near_list, table)
    )
    window = octant_window(far_list * ops + far_op)
    rows = leaves + halo if pair else leaves + 2 * halo
    listed = listed_pairs(near_list, device, pair, rows, halo)
    by_component = points.transpose(1, 0, 2)
    points_other = beside(by_component, 1, halo)

    counts = pl.pallas_call(
        functools.partial(counts_kernel, pair, octs),
        out_shape=jax.ShapeDtypeStruct((ops * slots, devices * slots), BF16),
        in_specs=[VMEM, VMEM],
        out_specs=VMEM,
        scratch_shapes=[pltpu.VMEM((ops, slots, devices * slots), F32)],
        compiler_params=params(4 if pair else 16),
        name="interaction_counts",
    )(window // ops, window % ops)

    density_now = density
    for step in range(ITERS):
        tables = lax.all_to_all(table, AXES, 0, 0, tiled=True)
        q_other = beside(density_now, 0, halo)
        near = near_start(pair, leaves, listed, by_component, points_other, density_now, q_other)
        last = step == ITERS - 1
        density_now, result = pl.pallas_call(
            functools.partial(later_kernel, pair, octs, last),
            out_shape=(field_shape, field_shape if last else table_shape),
            in_specs=[VMEM] * 9 + [HBM],
            out_specs=(VMEM, VMEM),
            scratch_shapes=[
                pltpu.VMEM(anterp.shape, BF16),
                pltpu.VMEM((ops, slots, nodes), F32),
                pltpu.VMEM((CHILDREN, slots, nodes), F32),
                pltpu.SemaphoreType.DMA,
            ],
            compiler_params=params(LATER_MIB),
            name="downward_upward",
        )(near, tables, counts, source, density_now, child_row, parent_row, translations, child_ops, in_hbm(anterp))
        if last:
            potential = result
        else:
            table = result
    return density_now, potential


def solution(mesh):
    rows = P(AXES, None)
    blocks = P(AXES, None, None)
    line = P(AXES)
    in_specs = (blocks, rows, rows, blocks, line, P(), line, rows, rows, rows, P())
    return jax.shard_map(shards, mesh=mesh, in_specs=in_specs, out_specs=(rows, rows), check_vma=False)
```

profile of v0, /device:TPU:0, one launch (start us, length us, event | category | flops | bytes accessed | tf_op | source)
XLA Modules:
  0.0 43.1 jit_solution(1957938044094187772)
XLA Ops:
  0.6 0.0 copy-start.2
  0.6 0.0 copy-start.8
  0.7 0.0 copy-start.9
  0.7 0.0 copy-start.7
  0.7 0.0 copy-start.6
  0.7 0.5 %collective-permute-start.1 = (f32[32,128]{1,0:T(8,128)}, f32[32,128]{1,0:T(8,128)S(1)}, u32[]{:S(2)}, u32[]{:S(2)}) collective-permute-start(f32[32,128]{1,0:T(8,128)} %q_ref.3), channel_id=1, source_target_pairs={{0,1},{1,0},{2,3},{3,2},{4,5},{5,4},{6,7},{7,6},{8,9},{9,8},{10,11... | collective-permute-start | bytes 49160 | tf_op jit(solution)/shard_map/ppermute | solution.py:339
  1.2 3.3 %upward_pass.1 = bf16[32,8,216]{2,1,0:T(8,128)(2,1)} custom-call(f32[32,128]{1,0:T(8,128)} %q_ref.3, s32[1,32]{1,0:T(1,128)} %bitcast.3, s32[1,32]{1,0:T(1,128)} %bitcast.6, bf16[32,216,128]{2,1,0:T(8,128)(2,1)} %anterp_hbm.5, bf16[8,216,216]{2,1,0:T(8,128)(2,1)} %child_ref.3), custom_call_target="tpu_custom_call" | custom-call | tf_op jit(solution)/shard_map/upward_pass/pallas_call | solution.py:393
  4.5 7.0 %all-to-all-start = ((bf16[32,8,216]{2,1,0:T(8,128)(2,1)}), bf16[32,8,216]{2,1,0:T(8,128)(2,1)S(1)}, u32[]{:S(2)}, u32[]{:S(2)}) async-start(bf16[32,8,216]{2,1,0:T(8,128)(2,1)} %upward_pass.1), calls=%async_computation | async-start | bytes 262144 | tf_op jit(solution)/shard_map/all_to_all | solution.py:431
  11.6 0.3 collective-permute-start.2
  11.9 0.3 collective-permute-start
  12.1 0.0 copy-done.7
  12.1 0.1 copy.13
  12.2 0.2 compare_reduce_fusion
  12.4 0.4 collective-permute-done.2
  12.8 0.4 interaction_counts.1.counts_ref
  13.2 0.0 copy-start
  13.2 0.0 copy-start.1
  13.3 0.0 copy-start.3
  13.3 0.0 copy-start.4
  13.3 0.0 copy-start.5
  13.3 0.0 collective-permute-done.1.q_other_ref
  13.3 0.0 collective-permute-done.points_other_ref
  13.3 0.0 copy-done.2
  13.3 8.2 %near_start.2.near_ref = f32[32,128]{1,0:T(8,128)S(1)} custom-call(f32[32,48]{1,0:T(8,128)S(1)} %convert_element_type.3.listed_ref, f32[3,32,128]{2,1,0:T(8,128)S(1)} %bitcast.10, f32[3,32,128]{2,1,0:T(8,128)S(1)} %collective-permute-done.points_other_ref, f32[32,128]{1,0:T(8,128)S(1)} %copy-done.2, f32[32,128]{1,0:T(8,128)S(1)} %collective-permute-done.1.q_other_ref), custom_call_target="tpu_custom_call" | custom-call | flops 60129542144 | bytes 1048576 | tf_op jit(solution)/shard_map/near_start/pallas_call | solution.py:183
  21.6 0.0 all-to-all-done.tables_ref
  21.6 4.4 %downward_upward.2 = (f32[32,128]{1,0:T(8,128)S(1)}, bf16[32,8,216]{2,1,0:T(8,128)(2,1)}) custom-call(f32[32,128]{1,0:T(8,128)S(1)} %near_start.2.near_ref, bf16[32,8,216]{2,1,0:T(8,128)(2,1)S(1)} %all-to-all-done.tables_ref, bf16[128,256]{1,0:T(8,128)(2,1)S(1)} %interaction_counts.1.counts_ref, f32[32,128]{1,0:T(8,128)S(1)} %copy-done.3, ...), custom_call_target="tpu_custom_call" | custom-call | tf_op jit(solution)/shard_map/downward_upward/pallas_call | solution.py:435
  26.0 0.3 collective-permute-start.3
  26.3 5.7 %all-to-all-start.1 = ((bf16[32,8,216]{2,1,0:T(8,128)(2,1)}), bf16[32,8,216]{2,1,0:T(8,128)(2,1)S(1)}, u32[]{:S(2)}, u32[]{:S(2)}) async-start(bf16[32,8,216]{2,1,0:T(8,128)(2,1)} %get-tuple-element.15), calls=%async_computation.1 | async-start | bytes 262144 | tf_op jit(solution)/shard_map/all_to_all | solution.py:431
  32.1 0.0 collective-permute-done.3.q_other_ref
  32.1 8.2 %near_start.3.near_ref = f32[32,128]{1,0:T(8,128)S(1)} custom-call(f32[32,48]{1,0:T(8,128)S(1)} %convert_element_type.3.listed_ref, f32[3,32,128]{2,1,0:T(8,128)S(1)} %bitcast.11, f32[3,32,128]{2,1,0:T(8,128)S(1)} %collective-permute-done.points_other_ref, f32[32,128]{1,0:T(8,128)S(1)} %get-tuple-element.14.q_ref, ...), custom_call_target="tpu_custom_call" | custom-call | flops 60129542144 | bytes 1048576 | tf_op jit(solution)/shard_map/near_start/pallas_call | solution.py:183
  40.3 0.0 all-to-all-done.1.tables_ref
  40.4 2.7 %downward_upward.3 = (f32[32,128]{1,0:T(8,128)}, f32[32,128]{1,0:T(8,128)}) custom-call(f32[32,128]{1,0:T(8,128)S(1)} %near_start.3.near_ref, bf16[32,8,216]{2,1,0:T(8,128)(2,1)S(1)} %all-to-all-done.1.tables_ref, bf16[128,256]{1,0:T(8,128)(2,1)S(1)} %interaction_counts.1.counts_ref, f32[32,128]{1,0:T(8,128)S(1)} %copy-done.3, ...), custom_call_target="tpu_custom_call" | custom-call | tf_op jit(solution)/shard_map/downward_upward/pallas_call | solution.py:435
  (12 shorter events, 0.1 us)
Async XLA Ops:
  0.6 12.7 %copy-start.2 = (f32[32,128]{1,0:T(8,128)S(1)}, f32[32,128]{1,0:T(8,128)}, u32[]{:S(2)}) copy-start(f32[32,128]{1,0:T(8,128)} %q_ref.3) | copy-start | bytes 49156
  0.6 10.9 %copy-start.8 = (s32[4,189]{1,0:T(4,128)S(1)}, s32[4,189]{1,0:T(4,128)}, u32[]{:S(2)}) copy-start(s32[4,189]{1,0:T(4,128)} %param.20) | copy-start | bytes 9076
  0.7 10.9 %copy-start.9 = (s32[4,189]{1,0:T(4,128)S(1)}, s32[4,189]{1,0:T(4,128)}, u32[]{:S(2)}) copy-start(s32[4,189]{1,0:T(4,128)} %param.19) | copy-start | bytes 9076
  0.7 11.5 %copy-start.7 = (s32[32,27]{1,0:T(8,128)S(1)}, s32[32,27]{1,0:T(8,128)}, u32[]{:S(2)}) copy-start(s32[32,27]{1,0:T(8,128)} %param.18) | copy-start | bytes 10372
  0.7 11.2 %copy-start.6 = (f32[32,3,128]{2,0,1:T(8,128)S(1)}, f32[32,3,128]{2,0,1:T(8,128)}, u32[]{:S(2)}) copy-start(f32[32,3,128]{2,0,1:T(8,128)} %param.11) | copy-start | bytes 147460
  0.7 12.6 %collective-permute-start.1 = (f32[32,128]{1,0:T(8,128)}, f32[32,128]{1,0:T(8,128)S(1)}, u32[]{:S(2)}, u32[]{:S(2)}) collective-permute-start(f32[32,128]{1,0:T(8,128)} %q_ref.3), channel_id=1, source_target_pairs={{0,1},{1,0},{2,3},{3,2},{4,5},{5,4},{6,7},{7,6},{8,9},{9,8},{10,11... | collective-permute-start | bytes 49160 | tf_op jit(solution)/shard_map/ppermute | solution.py:339
  4.5 17.0 %all-to-all-start = ((bf16[32,8,216]{2,1,0:T(8,128)(2,1)}), bf16[32,8,216]{2,1,0:T(8,128)(2,1)S(1)}, u32[]{:S(2)}, u32[]{:S(2)}) async-start(bf16[32,8,216]{2,1,0:T(8,128)(2,1)} %upward_pass.1), calls=%async_computation | async-start | bytes 262144 | tf_op jit(solution)/shard_map/all_to_all | solution.py:431
  11.6 1.2 %collective-permute-start.2 = (s32[4,189]{1,0:T(4,128)S(1)}, s32[4,189]{1,0:T(4,128)S(1)}, u32[]{:S(2)}, u32[]{:S(2)}) collective-permute-start(s32[4,189]{1,0:T(4,128)S(1)} %multiply_add_fusion), channel_id=1, source_target_pairs={{0,1},{1,0},{2,3},{3,2},{4,5},{5,4},{6,7},{7,6},{8,9},{9,8},{10,11... | collective-permute-start | bytes 9080 | tf_op jit(solution)/shard_map/ppermute | solution.py:339
  11.9 1.4 %collective-permute-start = (f32[3,32,128]{2,1,0:T(8,128)S(1)}, f32[3,32,128]{2,1,0:T(8,128)S(1)}, u32[]{:S(2)}, u32[]{:S(2)}) collective-permute-start(f32[3,32,128]{2,1,0:T(8,128)S(1)} %bitcast.9), channel_id=1, source_target_pairs={{0,1},{1,0},{2,3},{3,2},{4,5},{5,4},{6,7},{7,6},{8,9},{9,8},{10,11... | collective-permute-start | bytes 147464 | tf_op jit(solution)/shard_map/ppermute | solution.py:339
  13.2 8.3 %copy-start = (bf16[8,216,216]{2,1,0:T(8,128)(2,1)S(1)}, bf16[8,216,216]{2,1,0:T(8,128)(2,1)}, u32[]{:S(2)}) copy-start(bf16[8,216,216]{2,1,0:T(8,128)(2,1)} %child_ref.3) | copy-start | bytes 2239492
  13.2 8.3 %copy-start.1 = (bf16[16,216,216]{2,1,0:T(8,128)(2,1)S(1)}, bf16[16,216,216]{2,1,0:T(8,128)(2,1)}, u32[]{:S(2)}) copy-start(bf16[16,216,216]{2,1,0:T(8,128)(2,1)} %trans_ref.3) | copy-start | bytes 4478980
  13.3 8.3 %copy-start.3 = (f32[32,128]{1,0:T(8,128)S(1)}, f32[32,128]{1,0:T(8,128)}, u32[]{:S(2)}) copy-start(f32[32,128]{1,0:T(8,128)} %source_ref.3) | copy-start | bytes 49156
  13.3 8.3 %copy-start.4 = (s32[32]{0:T(128)S(1)}, s32[32]{0:T(128)}, u32[]{:S(2)}) copy-start(s32[32]{0:T(128)} %param.15) | copy-start | bytes 388
  13.3 8.3 %copy-start.5 = (s32[32]{0:T(128)S(1)}, s32[32]{0:T(128)}, u32[]{:S(2)}) copy-start(s32[32]{0:T(128)} %param.17) | copy-start | bytes 388
  26.0 6.1 %collective-permute-start.3 = (f32[32,128]{1,0:T(8,128)S(1)}, f32[32,128]{1,0:T(8,128)S(1)}, u32[]{:S(2)}, u32[]{:S(2)}) collective-permute-start(f32[32,128]{1,0:T(8,128)S(1)} %get-tuple-element.14.q_ref), channel_id=1, source_target_pairs={{0,1},{1,0},{2,3},{3,2},{4,5},{5,4},{6,7},{7,6},{8,9},{9,8},{10,11... | collective-permute-start | bytes 49160 | tf_op jit(solution)/shard_map/ppermute | solution.py:339
  26.3 14.0 %all-to-all-start.1 = ((bf16[32,8,216]{2,1,0:T(8,128)(2,1)}), bf16[32,8,216]{2,1,0:T(8,128)(2,1)S(1)}, u32[]{:S(2)}, u32[]{:S(2)}) async-start(bf16[32,8,216]{2,1,0:T(8,128)(2,1)} %get-tuple-element.15), calls=%async_computation.1 | async-start | bytes 262144 | tf_op jit(solution)/shard_map/all_to_all | solution.py:431
where the time goes:
time: 43.4 us; the launch traced here: 43.1 us
  Pallas kernels  27.3 us (63%)
  starting transfers between devices  14.1 us (32%)
  between operations  0.89 us (2%)
    pallas_call x2, Pallas kernels, near_start(): pl.pallas_call(functools.partial(near_kernel, pair, count), out_shape=jax...  16.5 us
    all_to_all x2, starting transfers between devices, shards(): tables = lax.all_to_all(table, AXES, 0, 0, tiled=True)  12.7 us
    pallas_call x2, Pallas kernels, shards(): pl.pallas_call(functools.partial(later_kernel, pair, octs, last), out_sha...  7.12 us
    pallas_call x1, Pallas kernels, shards(): pl.pallas_call(functools.partial(first_kernel, pair, octs), out_shape=tab...  3.34 us
    ppermute x4, starting transfers between devices, swap(): return lax.ppermute(array, 'gz', [(0, 1), (1, 0)])  1.41 us
  transfers between devices with their start and end apart: 6, of which 1 were waited for; matrix products, arithmetic and copies ran while one was open for 1% of the time, Pallas kernels for 47%

commit v1 on v0

--- a/solution.py
+++ b/solution.py
@@ -19,7 +19,8 @@
 
 BF16 = jnp.bfloat16
 F32 = jnp.float32
-UNROLL = 8
+UNROLL = 16
+MATRIX_LEAVES = 8
 M2L_LOOP = 2
 L2L_LOOP = 2
 CHUNKS = 2
@@ -108,9 +109,9 @@
         q_s[pl.ds(leaves + i, 1), :] = q_other_ref[pl.ds(leaf, 1), :]
         return carry
 
-    lax.fori_loop(first, stop, own, 0, unroll=4)
-    lax.fori_loop(stop, min(end, leaves), own_source, 0, unroll=4)
-    lax.fori_loop(0, max(end - leaves, 0), other, 0, unroll=4)
+    lax.fori_loop(first, stop, own, 0, unroll=16)
+    lax.fori_loop(stop, min(end, leaves), own_source, 0, unroll=16)
+    lax.fori_loop(0, max(end - leaves, 0), other, 0, unroll=13)
 
     def target(i, carry):
         rows = target_s[i]
@@ -203,13 +204,21 @@
     return jnp.where(index == code, 1.0, 0.0).astype(BF16)
 
 
-def leaf_multipoles(by_point, anterp_ref, first, count):
+def leaf_multipoles(q_ref, anterp_ref, first, count):
+    by_point = q_ref[...].T.astype(BF16)
+    nodes, leaves = anterp_ref.shape[1], by_point.shape[1]
     lane = lax.broadcasted_iota(jnp.int32, by_point.shape, 1)
-    mult = jnp.zeros((anterp_ref.shape[1], by_point.shape[1]), F32)
-    for leaf in range(0, count, 2):
+    mult = jnp.zeros((nodes, leaves), F32)
+    split = count * MATRIX_LEAVES // 16 // 2 * 2
+    for leaf in range(0, split, 2):
         maps = jnp.concatenate([anterp_ref[first + leaf], anterp_ref[first + leaf + 1]], 1)
         values = [jnp.where(lane == first + leaf + i, by_point, 0.0) for i in (0, 1)]
         mult = mult + dot(maps, jnp.concatenate(values, 0))
+    column = lax.broadcasted_iota(jnp.int32, mult.shape, 1)
+    for leaf in range(split, count):
+        values = q_ref[pl.ds(first + leaf, 1), :].astype(BF16).astype(F32)
+        sums = jnp.sum(anterp_ref[first + leaf].astype(F32) * values, axis=1, keepdims=True)
+        mult = jnp.where(column == first + leaf, sums, mult)
     return mult
 
 
@@ -253,7 +262,12 @@
     leaf_local = lax.dot_general(pick, back, (((0,), (0,)), ((), ())), preferred_element_type=F32)
     leaf_local = leaf_local.astype(BF16)
     maps_ready()
-    far = [dot(leaf_local[leaf : leaf + 1], anterp_ref[leaf]) for leaf in range(leaves)]
+    width = anterp_ref.shape[2]
+    far = []
+    for leaf in range(0, leaves, 2):
+        maps = jnp.concatenate([anterp_ref[leaf], anterp_ref[leaf + 1]], 1)
+        both = dot(leaf_local[leaf : leaf + 2], maps)
+        far += [both[:1, :width], both[1:, width:]]
     return jnp.concatenate(far, 0)
 
 
@@ -289,11 +303,9 @@
     for copy in small:
         copy.wait()
     code = leaf_codes(pair, octs, table_ref.shape[1], child_slot_s, parent_s)
-    by_point = q_s[...].T.astype(BF16)
-
     def take(i, mult):
         maps(i).wait()
-        return mult + leaf_multipoles(by_point, anterp_s, i * chunk, chunk)
+        return mult + leaf_multipoles(q_s, anterp_s, i * chunk, chunk)
 
     mult = lax.fori_loop(0, CHUNKS, take, jnp.zeros((anterp_s.shape[1], anterp_s.shape[0]), F32))
     child.wait()
@@ -312,7 +324,7 @@
     if last:
         other_out_ref[...] = potential
     else:
-        mult = leaf_multipoles(new_q.T.astype(BF16), anterp_s, 0, anterp_s.shape[0])
+        mult = leaf_multipoles(new_q_ref, anterp_s, 0, anterp_s.shape[0])
         octant_parts(mult, code, child_ref, other_out_ref)
 
 
@@ -407,8 +419,8 @@
         name="upward_pass",
     )(*map(in_hbm, (density, child_row, parent_row, anterp, child_ops)))
 
-    points, far_list, far_op, near_list, table = lax.optimization_barrier(
-        (points, far_list, far_op, near_list, table)
+    points, density_sent, far_list, far_op, near_list, table = lax.optimization_barrier(
+        (points, density, far_list, far_op, near_list, table)
     )
     window = octant_window(far_list * ops + far_op)
     rows = leaves + halo if pair else leaves + 2 * halo
@@ -429,7 +441,7 @@
     density_now = density
     for step in range(ITERS):
         tables = lax.all_to_all(table, AXES, 0, 0, tiled=True)
-        q_other = beside(density_now, 0, halo)
+        q_other = beside(density_now if step else density_sent, 0, halo)
         near = near_start(pair, leaves, listed, by_component, points_other, density_now, q_other)
         last = step == ITERS - 1
         density_now, result = pl.pallas_call(

time: 43.4 us -> 41.5 us (0.956)
  Pallas kernels: 27.3 us -> 24.7 us
  waiting for transfers between devices: 0.37 us -> 1.14 us
    pallas_call x2, Pallas kernels: 16.5 us -> 14.5 us  [near_start(): pl.pallas_call(functools.partial(near_kernel, pair, count), out_shape=jax...]
    all_to_all x2, waiting for transfers between devices: 0.01 us -> 0.97 us  [shards(): tables = lax.all_to_all(table, AXES, 0, 0, tiled=True)]
    pallas_call x2, Pallas kernels: 7.12 us -> 6.42 us  [shards(): pl.pallas_call(functools.partial(later_kernel, pair, octs, last), out_sha...]
  transfers between devices with their start and end apart: 6 -> 6, of which waited for: 1 -> 3; matrix products, arithmetic and copies ran while one was open for 1% -> 1% of each run, Pallas kernels for 47% -> 36%
where the time goes in v1:
time: 41.5 us; the launch traced here: 41.2 us
  Pallas kernels  24.7 us (60%)
  starting transfers between devices  14.2 us (34%)
  waiting for transfers between devices  1.14 us (3%)
  between operations  0.87 us (2%)
    pallas_call x2, Pallas kernels, near_start(): pl.pallas_call(functools.partial(near_kernel, pair, count), out_shape=jax...  14.5 us
    all_to_all x2, starting transfers between devices, shards(): tables = lax.all_to_all(table, AXES, 0, 0, tiled=True)  13.1 us
    pallas_call x2, Pallas kernels, shards(): pl.pallas_call(functools.partial(later_kernel, pair, octs, last), out_sha...  6.42 us
    pallas_call x1, Pallas kernels, shards(): pl.pallas_call(functools.partial(first_kernel, pair, octs), out_shape=tab...  3.33 us
    ppermute x4, starting transfers between devices, swap(): return lax.ppermute(array, 'gz', [(0, 1), (1, 0)])  1.14 us
    all_to_all x2, waiting for transfers between devices, shards(): tables = lax.all_to_all(table, AXES, 0, 0, tiled=True)  0.97 us
  transfers between devices with their start and end apart: 6, of which 3 were waited for; matrix products, arithmetic and copies ran while one was open for 1% of the time, Pallas kernels for 36%

profile of v1, /device:TPU:0, one launch (start us, length us, event | category | flops | bytes accessed | tf_op | source)
XLA Modules:
  0.0 41.2 jit_solution(13800220298908521138)
XLA Ops:
  0.6 0.0 copy-start.2
  0.6 0.0 copy-start.8
  0.7 0.0 copy-start.9
  0.7 0.0 copy-start.7
  0.7 0.0 copy-start.6
  0.7 3.3 %upward_pass.1 = bf16[32,8,216]{2,1,0:T(8,128)(2,1)} custom-call(f32[32,128]{1,0:T(8,128)} %q_ref.3, s32[1,32]{1,0:T(1,128)} %bitcast.3, s32[1,32]{1,0:T(1,128)} %bitcast.6, bf16[32,216,128]{2,1,0:T(8,128)(2,1)} %anterp_hbm.5, bf16[8,216,216]{2,1,0:T(8,128)(2,1)} %child_ref.3), custom_call_target="tpu_custom_call" | custom-call | tf_op jit(solution)/shard_map/upward_pass/pallas_call | solution.py:405
  4.0 7.3 %all-to-all-start = ((bf16[32,8,216]{2,1,0:T(8,128)(2,1)}), bf16[32,8,216]{2,1,0:T(8,128)(2,1)S(1)}, u32[]{:S(2)}, u32[]{:S(2)}) async-start(bf16[32,8,216]{2,1,0:T(8,128)(2,1)} %upward_pass.1), calls=%async_computation | async-start | bytes 262144 | tf_op jit(solution)/shard_map/all_to_all | solution.py:443
  11.4 0.3 collective-permute-start.2
  11.7 0.0 copy-done.2
  11.7 0.3 collective-permute-start.1
  12.0 0.3 collective-permute-start
  12.2 0.0 copy-done.7
  12.2 0.1 copy.13
  12.3 0.2 compare_reduce_fusion
  12.5 0.1 collective-permute-done.2
  12.6 0.4 %interaction_counts.1.counts_ref = bf16[128,256]{1,0:T(8,128)(2,1)S(1)} custom-call(s32[8,189]{1,0:T(8,128)S(1)} %get-tuple-element.19.far_list_ref, s32[8,189]{1,0:T(8,128)S(1)} %get-tuple-element.18.far_op_ref), custom_call_target="tpu_custom_call" | custom-call | tf_op jit(solution)/shard_map/interaction_counts/pallas_call | solution.py:431
  13.1 0.0 copy-start
  13.1 0.0 copy-start.1
  13.1 0.0 copy-start.3
  13.1 0.0 copy-start.4
  13.1 0.0 copy-start.5
  13.1 0.0 collective-permute-done.1.q_other_ref
  13.1 0.1 collective-permute-done.points_other_ref
  13.2 7.2 %near_start.2.near_ref = f32[32,128]{1,0:T(8,128)S(1)} custom-call(f32[32,48]{1,0:T(8,128)S(1)} %convert_element_type.3.listed_ref, f32[3,32,128]{2,1,0:T(8,128)S(1)} %bitcast.10, f32[3,32,128]{2,1,0:T(8,128)S(1)} %collective-permute-done.points_other_ref, f32[32,128]{1,0:T(8,128)S(1)} %copy-done.2, f32[32,128]{1,0:T(8,128)S(1)} %collective-permute-done.1.q_other_ref), custom_call_target="tpu_custom_call" | custom-call | flops 60129542144 | bytes 1048576 | tf_op jit(solution)/shard_map/near_start/pallas_call | solution.py:184
  20.4 0.0 all-to-all-done.tables_ref
  20.5 3.9 %downward_upward.2 = (f32[32,128]{1,0:T(8,128)S(1)}, bf16[32,8,216]{2,1,0:T(8,128)(2,1)}) custom-call(f32[32,128]{1,0:T(8,128)S(1)} %near_start.2.near_ref, bf16[32,8,216]{2,1,0:T(8,128)(2,1)S(1)} %all-to-all-done.tables_ref, bf16[128,256]{1,0:T(8,128)(2,1)S(1)} %interaction_counts.1.counts_ref, f32[32,128]{1,0:T(8,128)S(1)} %copy-done.3, ...), custom_call_target="tpu_custom_call" | custom-call | tf_op jit(solution)/shard_map/downward_upward/pallas_call | solution.py:447
  24.4 0.3 collective-permute-start.3
  24.8 5.7 %all-to-all-start.1 = ((bf16[32,8,216]{2,1,0:T(8,128)(2,1)}), bf16[32,8,216]{2,1,0:T(8,128)(2,1)S(1)}, u32[]{:S(2)}, u32[]{:S(2)}) async-start(bf16[32,8,216]{2,1,0:T(8,128)(2,1)} %get-tuple-element.17), calls=%async_computation.1 | async-start | bytes 262144 | tf_op jit(solution)/shard_map/all_to_all | solution.py:443
  30.5 0.0 collective-permute-done.3.q_other_ref
  30.5 7.2 %near_start.3.near_ref = f32[32,128]{1,0:T(8,128)S(1)} custom-call(f32[32,48]{1,0:T(8,128)S(1)} %convert_element_type.3.listed_ref, f32[3,32,128]{2,1,0:T(8,128)S(1)} %bitcast.11, f32[3,32,128]{2,1,0:T(8,128)S(1)} %collective-permute-done.points_other_ref, f32[32,128]{1,0:T(8,128)S(1)} %get-tuple-element.16.q_ref, ...), custom_call_target="tpu_custom_call" | custom-call | flops 60129542144 | bytes 1048576 | tf_op jit(solution)/shard_map/near_start/pallas_call | solution.py:184
  37.8 1.0 %all-to-all-done.1.tables_ref = bf16[32,8,216]{2,1,0:T(8,128)(2,1)S(1)} async-done(((bf16[32,8,216]{2,1,0:T(8,128)(2,1)}), bf16[32,8,216]{2,1,0:T(8,128)(2,1)S(1)}, u32[]{:S(2)}, u32[]{:S(2)}) %all-to-all-start.1) | async-done | bytes 110624 | tf_op jit(solution)/shard_map/all_to_all | solution.py:443
  38.7 2.5 %downward_upward.3 = (f32[32,128]{1,0:T(8,128)}, f32[32,128]{1,0:T(8,128)}) custom-call(f32[32,128]{1,0:T(8,128)S(1)} %near_start.3.near_ref, bf16[32,8,216]{2,1,0:T(8,128)(2,1)S(1)} %all-to-all-done.1.tables_ref, bf16[128,256]{1,0:T(8,128)(2,1)S(1)} %interaction_counts.1.counts_ref, f32[32,128]{1,0:T(8,128)S(1)} %copy-done.3, ...), custom_call_target="tpu_custom_call" | custom-call | tf_op jit(solution)/shard_map/downward_upward/pallas_call | solution.py:447
  (12 shorter events, 0.1 us)
Async XLA Ops:
  0.6 11.1 %copy-start.2 = (f32[32,128]{1,0:T(8,128)S(1)}, f32[32,128]{1,0:T(8,128)}, u32[]{:S(2)}) copy-start(f32[32,128]{1,0:T(8,128)} %q_ref.3) | copy-start | bytes 49156
  0.6 10.7 %copy-start.8 = (s32[4,189]{1,0:T(4,128)S(1)}, s32[4,189]{1,0:T(4,128)}, u32[]{:S(2)}) copy-start(s32[4,189]{1,0:T(4,128)} %param.20) | copy-start | bytes 9076
  0.7 10.7 %copy-start.9 = (s32[4,189]{1,0:T(4,128)S(1)}, s32[4,189]{1,0:T(4,128)}, u32[]{:S(2)}) copy-start(s32[4,189]{1,0:T(4,128)} %param.19) | copy-start | bytes 9076
  0.7 11.5 %copy-start.7 = (s32[32,27]{1,0:T(8,128)S(1)}, s32[32,27]{1,0:T(8,128)}, u32[]{:S(2)}) copy-start(s32[32,27]{1,0:T(8,128)} %param.18) | copy-start | bytes 10372
  0.7 11.3 %copy-start.6 = (f32[32,3,128]{2,0,1:T(8,128)S(1)}, f32[32,3,128]{2,0,1:T(8,128)}, u32[]{:S(2)}) copy-start(f32[32,3,128]{2,0,1:T(8,128)} %param.11) | copy-start | bytes 147460
  4.0 16.4 %all-to-all-start = ((bf16[32,8,216]{2,1,0:T(8,128)(2,1)}), bf16[32,8,216]{2,1,0:T(8,128)(2,1)S(1)}, u32[]{:S(2)}, u32[]{:S(2)}) async-start(bf16[32,8,216]{2,1,0:T(8,128)(2,1)} %upward_pass.1), calls=%async_computation | async-start | bytes 262144 | tf_op jit(solution)/shard_map/all_to_all | solution.py:443
  11.4 1.2 %collective-permute-start.2 = (s32[4,189]{1,0:T(4,128)S(1)}, s32[4,189]{1,0:T(4,128)S(1)}, u32[]{:S(2)}, u32[]{:S(2)}) collective-permute-start(s32[4,189]{1,0:T(4,128)S(1)} %multiply_add_fusion), channel_id=1, source_target_pairs={{0,1},{1,0},{2,3},{3,2},{4,5},{5,4},{6,7},{7,6},{8,9},{9,8},{10,11... | collective-permute-start | bytes 9080 | tf_op jit(solution)/shard_map/ppermute | solution.py:351
  11.7 1.4 %collective-permute-start.1 = (f32[32,128]{1,0:T(8,128)S(1)}, f32[32,128]{1,0:T(8,128)S(1)}, u32[]{:S(2)}, u32[]{:S(2)}) collective-permute-start(f32[32,128]{1,0:T(8,128)S(1)} %copy-done.2), channel_id=1, source_target_pairs={{0,1},{1,0},{2,3},{3,2},{4,5},{5,4},{6,7},{7,6},{8,9},{9,8},{10,11... | collective-permute-start | bytes 49160 | tf_op jit(solution)/shard_map/ppermute | solution.py:351
  12.0 1.2 %collective-permute-start = (f32[3,32,128]{2,1,0:T(8,128)S(1)}, f32[3,32,128]{2,1,0:T(8,128)S(1)}, u32[]{:S(2)}, u32[]{:S(2)}) collective-permute-start(f32[3,32,128]{2,1,0:T(8,128)S(1)} %bitcast.9), channel_id=1, source_target_pairs={{0,1},{1,0},{2,3},{3,2},{4,5},{5,4},{6,7},{7,6},{8,9},{9,8},{10,11... | collective-permute-start | bytes 147464 | tf_op jit(solution)/shard_map/ppermute | solution.py:351
  13.1 7.4 %copy-start = (bf16[8,216,216]{2,1,0:T(8,128)(2,1)S(1)}, bf16[8,216,216]{2,1,0:T(8,128)(2,1)}, u32[]{:S(2)}) copy-start(bf16[8,216,216]{2,1,0:T(8,128)(2,1)} %child_ref.3) | copy-start | bytes 2239492
  13.1 7.4 %copy-start.1 = (bf16[16,216,216]{2,1,0:T(8,128)(2,1)S(1)}, bf16[16,216,216]{2,1,0:T(8,128)(2,1)}, u32[]{:S(2)}) copy-start(bf16[16,216,216]{2,1,0:T(8,128)(2,1)} %trans_ref.3) | copy-start | bytes 4478980
  13.1 7.4 %copy-start.3 = (f32[32,128]{1,0:T(8,128)S(1)}, f32[32,128]{1,0:T(8,128)}, u32[]{:S(2)}) copy-start(f32[32,128]{1,0:T(8,128)} %source_ref.3) | copy-start | bytes 49156
  13.1 7.4 %copy-start.4 = (s32[32]{0:T(128)S(1)}, s32[32]{0:T(128)}, u32[]{:S(2)}) copy-start(s32[32]{0:T(128)} %param.15) | copy-start | bytes 388
  13.1 7.4 %copy-start.5 = (s32[32]{0:T(128)S(1)}, s32[32]{0:T(128)}, u32[]{:S(2)}) copy-start(s32[32]{0:T(128)} %param.17) | copy-start | bytes 388
  24.4 6.1 %collective-permute-start.3 = (f32[32,128]{1,0:T(8,128)S(1)}, f32[32,128]{1,0:T(8,128)S(1)}, u32[]{:S(2)}, u32[]{:S(2)}) collective-permute-start(f32[32,128]{1,0:T(8,128)S(1)} %get-tuple-element.16.q_ref), channel_id=1, source_target_pairs={{0,1},{1,0},{2,3},{3,2},{4,5},{5,4},{6,7},{7,6},{8,9},{9,8},{10,11... | collective-permute-start | bytes 49160 | tf_op jit(solution)/shard_map/ppermute | solution.py:351
  24.8 14.0 %all-to-all-start.1 = ((bf16[32,8,216]{2,1,0:T(8,128)(2,1)}), bf16[32,8,216]{2,1,0:T(8,128)(2,1)S(1)}, u32[]{:S(2)}, u32[]{:S(2)}) async-start(bf16[32,8,216]{2,1,0:T(8,128)(2,1)} %get-tuple-element.17), calls=%async_computation.1 | async-start | bytes 262144 | tf_op jit(solution)/shard_map/all_to_all | solution.py:443
